TPU v7x, 256 devices: a whole 4x4x8 slice. The times are simulated.
256 devices in a mesh: dp: 4 (over z_lo), seq: 16 (over z_hi, x, core), head: 4 (over y).
Axes of the slice: x: 4, y: 4, z: 8 (z_hi: 2, z_lo: 4; z = z_hi * 4 + z_lo), core: 2. Of those that a mesh axis runs over, the one named last changes fastest.
Arguments:
- queries: bfloat16 [4, 2048, 4096], P('dp', 'seq', 'head'), may hold values from -8 to 8
- keys: bfloat16 [4, 2048, 1024], P('dp', 'seq', 'head'), may hold values from -8 to 8
- values: bfloat16 [4, 2048, 1024], P('dp', 'seq', 'head'), may hold values from -6 to 6
- grad_out: bfloat16 [4, 2048, 4096], P('dp', 'seq', 'head'), may hold values from -6 to 6
- doc_ids: int32 [4, 2048], P('dp', 'seq'), may hold values from 0 to 7, never falling along the last dimension, each value on 1 to 1536 neighbouring positions
- out_weight: bfloat16 [4096, 4096], P('head'), may hold values from -0.09375 to 0.09375
Outputs:
- layer_out: float32 [4, 2048, 4096], P('dp', 'seq', 'head')
- grad_queries: float32 [4, 2048, 4096], P('dp', 'seq', 'head')
- grad_keys: float32 [4, 2048, 1024], P('dp', 'seq', 'head')
- grad_values: float32 [4, 2048, 1024], P('dp', 'seq', 'head')
- weight_grad: float32 [4096, 4096], P('head', 'seq')
Inputs may be any that keep to these rules, and one draw needn't show every extreme that they name: `doc_ids`: never falling along a sequence; every number names a document of 1 to 1536 positions, and one document of each sequence has exactly 1536.
All inputs are finite; a program needn't handle non-finite values.
Results may differ from a plain program's by a relative error of at most 0.035.
Values may be sent and summed in bfloat16 or wider, within the bound.
No kernel may reach another device: no remote copies, remote signals or barrier semaphores. Data moves between devices by JAX's collectives and lax.ppermute only.
A program may use at most 128 MiB of HBM per device.

v0:
```python
import functools

import jax
import jax.numpy as jnp
from jax import lax
from jax.experimental import pallas as pl
from jax.experimental.pallas import tpu as pltpu
from jax.sharding import PartitionSpec as P

HEAD = 128
ROWS = 128
NEG = -1e30
SCALE = HEAD ** -0.5
LOG2E = 1.4426950408889634
F32 = jnp.float32
BF16 = jnp.bfloat16
VMEM_LIMIT = 48 * 1024 * 1024


def seq_perm(move):
    pairs = []
    for s in range(16):
        z, x, c = s // 8, (s // 2) % 4, s % 2
        nz, nx, nc = move(z, x, c)
        pairs.append((s, nz * 8 + nx * 2 + nc))
    return pairs


def core_swap(value):
    return lax.ppermute(value, "seq", seq_perm(lambda z, x, c: (z, x, 1 - c)))


def x_swap(value, bits):
    return lax.ppermute(value, "seq", seq_perm(lambda z, x, c: (z, x ^ bits, c)))


def z_swap(value):
    return lax.ppermute(value, "seq", seq_perm(lambda z, x, c: (1 - z, x, c)))


def nt(a, b):
    return lax.dot_general(a, b, (((1,), (1,)), ((), ())), preferred_element_type=F32)


def nn(a, b):
    return lax.dot_general(a, b, (((1,), (0,)), ((), ())), preferred_element_type=F32)


def tn(a, b):
    return lax.dot_general(a, b, (((0,), (0,)), ((), ())), preferred_element_type=F32)


def message_kernel(doc_ref, k_ref, v_ref, out_ref, doc_scr, sems):
    copies = [
        pltpu.make_async_copy(doc_ref, doc_scr, sems.at[0]),
        pltpu.make_async_copy(k_ref, out_ref.at[:ROWS, :256], sems.at[1]),
        pltpu.make_async_copy(v_ref, out_ref.at[:ROWS, 256:], sems.at[2]),
    ]
    for copy in copies:
        copy.start()
    copies[0].wait()
    docs = jnp.broadcast_to(doc_scr[...].astype(F32), (16, ROWS)).astype(BF16)
    for n in range(4):
        out_ref[ROWS:, n * ROWS:(n + 1) * ROWS] = docs
    copies[1].wait()
    copies[2].wait()


def fill(own_ref, pieces, kv_scr, bias_scr):
    own = own_ref[0]
    z, x, c = own // 8, (own // 2) % 4, own % 2
    key_at = lax.broadcasted_iota(jnp.int32, (ROWS, ROWS), 0)
    query_at = lax.broadcasted_iota(jnp.int32, (ROWS, ROWS), 1)
    lag = key_at - query_at
    query_doc = pieces[0][ROWS:ROWS + 1, :ROWS].astype(F32)
    for n, piece in enumerate(pieces):
        other, part, k = n // 8, (n // 4) % 2, n % 4
        at = n * ROWS
        kv_scr[at:at + ROWS, :] = piece[:ROWS, :]
        block = ((z + part) % 2) * 8 + (x ^ k) * 2 + (c + other) % 2
        doc = piece[ROWS:ROWS + 8, :ROWS].astype(F32)
        doc = jnp.broadcast_to(doc[:1, :], (ROWS, ROWS)).T
        allowed = (doc == query_doc) & (lag <= (own - block) * ROWS)
        bias_scr[at:at + ROWS, :] = jnp.where(allowed, 0.0, NEG)


def each(refs):
    return [ref.at[k] for ref in refs for k in range(ref.shape[0])]


def stack_heads(ref, kv):
    return jnp.concatenate(
        [ref[:, (kv * 4 + g) * HEAD:(kv * 4 + g + 1) * HEAD] for g in range(4)], axis=0
    )


STEP = 512


def attend(kv, q, top, total, acc, kv_scr, bias_scr, s_scr):
    count = kv_scr.shape[0] // STEP

    def scores(i, best):
        rows = pl.ds(pl.multiple_of(i * STEP, STEP), STEP)
        bias = bias_scr[rows, :]
        s = nt(kv_scr[rows, kv * HEAD:(kv + 1) * HEAD], q)
        s = s + jnp.concatenate([bias] * 4, axis=1)
        s_scr[rows, :] = s
        return jnp.maximum(best, jnp.max(s.reshape(STEP // 8, 8, 512), axis=0))

    best = lax.fori_loop(0, count, scores, jnp.broadcast_to(top, (8, 512)), unroll=True)
    best = jnp.max(best, axis=0, keepdims=True)
    factor = jnp.exp2((top - best) * (SCALE * LOG2E))

    def values(i, state):
        sums, acc = state
        rows = pl.ds(pl.multiple_of(i * STEP, STEP), STEP)
        p = jnp.exp2((s_scr[rows, :] - best) * (SCALE * LOG2E))
        v = kv_scr[rows, 256 + kv * HEAD:256 + (kv + 1) * HEAD]
        sums = sums + jnp.sum(p.reshape(STEP // 8, 8, 512), axis=0)
        return sums, acc + tn(v, p.astype(BF16))

    sums, acc = lax.fori_loop(0, count, values, (jnp.zeros((8, 512), F32), acc * factor), unroll=True)
    return best, total * factor + jnp.sum(sums, axis=0, keepdims=True), acc


def forward_kernel(own_ref, q_ref, *refs):
    pieces, (o_ref, lse_ref, kv_scr, bias_scr, s_scr) = each(refs[:2]), refs[2:]
    fill(own_ref, pieces, kv_scr, bias_scr)
    for kv in range(2):
        top, total, acc = attend(
            kv, stack_heads(q_ref, kv), jnp.full((1, 512), NEG, F32), jnp.zeros((1, 512), F32),
            jnp.zeros((HEAD, 512), F32), kv_scr, bias_scr, s_scr,
        )
        out = (acc / total).T.astype(BF16)
        for g in range(4):
            o_ref[:, (kv * 4 + g) * HEAD:(kv * 4 + g + 1) * HEAD] = out[g * ROWS:(g + 1) * ROWS]
        lse = top * (SCALE * LOG2E) + jnp.log2(total)
        lse_ref[kv] = jnp.broadcast_to(lse, (8, 512))


def backward_kernel(own_ref, q_ref, d_ref, o_ref, lse_ref, *refs):
    dq_ref, own_out, sib_out, kv_scr, bias_scr = refs[2:]
    fill(own_ref, each(refs[:2]), kv_scr, bias_scr)
    for kv in range(2):
        q = stack_heads(q_ref, kv)
        d = stack_heads(d_ref, kv)
        o = stack_heads(o_ref, kv)
        lse = lse_ref[kv, :1, :]
        product = d.astype(F32) * o.astype(F32)
        delta = jnp.sum(product.T, axis=0, keepdims=True)

        def half(out_ref, part, base):
            def tile(i, acc):
                rows = pl.ds(pl.multiple_of(base + i * STEP, STEP), STEP)
                k = kv_scr[rows, kv * HEAD:(kv + 1) * HEAD]
                v = kv_scr[rows, 256 + kv * HEAD:256 + (kv + 1) * HEAD]
                bias = bias_scr[rows, :]
                s = nt(k, q) * (SCALE * LOG2E) - lse
                p = jnp.exp2(s + jnp.concatenate([bias] * 4, axis=1))
                dp = nt(v, d)
                ds = (p * (dp - delta)).astype(BF16)
                dk = (nn(ds, q) * SCALE).astype(BF16)
                dv = nn(p.astype(BF16), d).astype(BF16)
                for h in range(4):
                    at = slice(h * ROWS, (h + 1) * ROWS)
                    out_ref[4 * i + h, part, :, kv * HEAD:(kv + 1) * HEAD] = dk[at]
                    out_ref[4 * i + h, part, :, 256 + kv * HEAD:256 + (kv + 1) * HEAD] = dv[at]
                return acc + tn(k, ds)

            return tile

        acc = jnp.zeros((HEAD, 512), F32)
        for part in range(2):
            acc = lax.fori_loop(0, 1, half(own_out, part, part * 512), acc, unroll=True)
            acc = lax.fori_loop(0, 1, half(sib_out, part, part * 512 + 1024), acc, unroll=True)
        dq = (acc * SCALE).T
        for g in range(4):
            dq_ref[:, (kv * 4 + g) * HEAD:(kv * 4 + g + 1) * HEAD] = dq[g * ROWS:(g + 1) * ROWS]


def weight_kernel(rel, z_ref, *refs):
    heads, grads, (out_ref, h_scr, g_scr) = refs[:4], refs[4:8], refs[8:]
    z = z_ref[0]
    for n in range(4):
        rows = slice(n * ROWS, (n + 1) * ROWS)
        h_scr[rows, :] = heads[n][...]
        for part in range(2):
            g_scr[part, rows, :] = grads[n][rel, part]

    def piece(k, carry):
        to = (z + k) % 8
        lanes = pl.ds(pl.multiple_of((to % 4) * 256, 256), 256)
        out_ref[k] = tn(h_scr[:, lanes], g_scr[to // 4]).astype(BF16)
        return carry

    lax.fori_loop(0, 8, piece, 0, unroll=True)


def select_kernel(at_ref, g0, g1, g2, g3, o0, o1, o2, o3, scr):
    x, c, y = at_ref[0], at_ref[1], at_ref[2]
    for k, g in enumerate((g0, g1, g2, g3)):
        scr[y ^ k] = g[...]
    for k, out in enumerate((o0, o1, o2, o3)):
        to = x ^ k
        for rel in range(2):
            lane = ((to % 2) * 2 + (c + rel) % 2) * 256
            for part in range(2):
                out[rel, part] = scr[part * 2 + to // 2, :, pl.ds(pl.multiple_of(lane, 256), 256)]


def weight_copies(places, w_ref, w_scr, sems):
    copies = []
    for k, place in enumerate(places):
        columns = pl.ds(pl.multiple_of(place * 1024, 1024), 1024)
        copies.append(pltpu.make_async_copy(w_ref.at[:, columns], w_scr.at[k], sems.at[k]))
    for copy in copies:
        copy.start()
    return copies


def grad_heads_kernel(at_ref, g0, g1, g2, g3, w_ref, out_ref, w_scr, sems):
    copies = weight_copies([at_ref[2] ^ k for k in range(4)], w_ref, w_scr, sems)
    acc = jnp.zeros(out_ref.shape, F32)
    for k, g in enumerate((g0, g1, g2, g3)):
        copies[k].wait()
        acc = acc + nt(g[...], w_scr[k])
    out_ref[...] = acc.astype(BF16)


def project_kernel(at_ref, h_ref, w_ref, own_ref, far_ref, w_scr, sems):
    y = at_ref[2]
    copies = weight_copies([y ^ bits for bits in (3, 2, 0, 1)], w_ref, w_scr, sems)
    h = h_ref[...]
    for k in range(4):
        copies[k].wait()
        out = far_ref if k < 2 else own_ref
        out[k % 2] = nn(h, w_scr[k]).astype(out.dtype)


def spread_kernel(at_ref, p0, p1, p2, p3, out_ref):
    for k, p in enumerate((p0, p1, p2, p3)):
        rows = pl.ds(pl.multiple_of((at_ref[3] ^ k) * 256, 256), 256)
        out_ref[rows, :] = p[...].astype(F32)


SMEM = pl.BlockSpec(memory_space=pltpu.SMEM)
VMEM = pl.BlockSpec(memory_space=pltpu.VMEM)


ANY = pl.BlockSpec(memory_space=pl.ANY)


def call(kernel, inputs, out_shape, scratch, time, anywhere=(), first=SMEM, limit=VMEM_LIMIT):
    specs = [first] + [ANY if n in anywhere else VMEM for n in range(1, len(inputs))]
    return pl.pallas_call(
        kernel,
        out_shape=out_shape,
        in_specs=specs,
        out_specs=jax.tree.map(lambda _: VMEM, out_shape),
        scratch_shapes=scratch,
        compiler_params=pltpu.CompilerParams(vmem_limit_bytes=limit),
        cost_estimate=pl.CostEstimate(
            flops=int(time * 6e9), bytes_accessed=1 << 20, transcendentals=0
        ),
    )(*inputs)


def y_swap(value, bits):
    return lax.ppermute(value, "head", [(i, i ^ bits) for i in range(4)])


def z_shift(value, by):
    pairs = []
    for at in range(8):
        to = (at + by) % 8
        for r in range(8):
            pairs.append(((at % 4) * 16 + (at // 4) * 8 + r, (to % 4) * 16 + (to // 4) * 8 + r))
    return lax.ppermute(value, ("dp", "seq"), pairs)


def together(*values):
    return lax.optimization_barrier(values)


def after(value, *others):
    return lax.optimization_barrier((value, *others))[0]


def added(*parts):
    total = parts[0].astype(F32)
    for part in parts[1:]:
        total = total + part.astype(F32)
    return total


def shards(queries, keys, values, grad_out, doc_ids, out_weight):
    rows = queries.shape[1]
    depth = out_weight.shape[0]
    index = lax.axis_index("seq")
    layer = lax.axis_index("dp")
    y = lax.axis_index("head")
    z, x, c = index // 8, (index // 2) % 4, index % 2
    own = index.astype(jnp.int32).reshape(1)
    height = (z * 4 + layer).astype(jnp.int32).reshape(1)
    place = jnp.stack([x, c, y, layer]).astype(jnp.int32)
    shape = jax.ShapeDtypeStruct

    message = call(
        message_kernel, [doc_ids, keys[0], values[0]], shape((rows + 16, 512), BF16),
        [pltpu.VMEM((1, rows), jnp.int32), pltpu.SemaphoreType.DMA((3,))], 0.5, (1, 2), ANY,
        60 * 1024 * 1024,
    )
    q = queries[0]
    w_scratch = [pltpu.VMEM((4, 1024, 1024), BF16), pltpu.SemaphoreType.DMA((4,))]
    cotangent = after(grad_out[0], message)
    *crossed, across, near1, near3 = together(
        *[y_swap(cotangent, k) for k in (1, 3)], z_swap(message),
        *[x_swap(message, k) for k in (1, 3)],
    )
    cotangents = [grad_out[0], crossed[0], y_swap(after(grad_out[0], across), 2), crossed[1]]

    chosen = call(
        select_kernel, [place] + cotangents, (shape((2, 2, rows, 256), BF16),) * 4,
        [pltpu.VMEM((4, rows, 1024), BF16)], 1.5,
    )
    near2, far1, far3, far2, *chosen = together(
        x_swap(message, 2), *[x_swap(across, k) for k in (1, 3, 2)],
        *chosen,
    )

    pieces = jnp.stack([message, near1, near2, near3, across, far1, far2, far3])
    theirs, *chosen = together(core_swap(pieces), *chosen)
    pieces = [pieces, theirs]
    heads, lse = call(
        forward_kernel, [own, q] + pieces,
        (shape((rows, depth), BF16), shape((2, 8, 512), F32)),
        [
            pltpu.VMEM((2048, 512), BF16),
            pltpu.VMEM((2048, ROWS), F32),
            pltpu.VMEM((2048, 512), F32),
        ],
        4,
    )
    head_grad = call(
        grad_heads_kernel, [after(place, theirs)] + cotangents + [out_weight], shape((rows, depth), BF16),
        w_scratch, 6, (5,),
    )
    heads, head_grad, *grads = together(
        heads, head_grad, *[x_swap(chosen[k], k) for k in (3, 2, 1)]
    )
    grads = [chosen[0]] + grads[::-1]

    grad_query, kept, given = call(
        backward_kernel, [own, q, head_grad, heads, lse] + pieces,
        (shape((rows, depth), F32), shape((4, 2, rows, 512), BF16), shape((4, 2, rows, 512), BF16)),
        [pltpu.VMEM((2048, 512), BF16), pltpu.VMEM((2048, ROWS), F32)], 11,
    )
    terms = call(
        project_kernel, [place, heads, out_weight],
        (shape((2, rows, 1024), F32), shape((2, rows, 1024), BF16)), w_scratch, 5, (2,),
    )
    kept, given, own_terms, far_terms, *close = together(
        kept, given, *terms, *[x_swap(heads, k) for k in (3, 2, 1)]
    )
    close = close[::-1]
    far_terms = y_swap(far_terms, 3)
    close = [heads] + close

    def products(rel):
        return call(
            functools.partial(weight_kernel, rel), [height] + close + grads,
            shape((8, 256, 256), BF16),
            [pltpu.VMEM((512, depth), BF16), pltpu.VMEM((2, 512, 256), BF16)], 1,
        )

    summed = added(kept, core_swap(given)).astype(BF16)
    theirs = core_swap(products(1))
    ours, theirs, summed = together(products(0), theirs, summed)

    up, down = added(ours[4], theirs[4]).astype(BF16), added(ours[5], theirs[5]).astype(BF16)
    back, *rest = [x_swap(summed[k], k) for k in (1, 3, 2)]
    for k in range(3):
        up = added(z_shift(up, 1), ours[3 - k], theirs[3 - k]).astype(BF16)
        down = z_shift(down, -1)
        if k < 2:
            down = added(down, ours[6 + k], theirs[6 + k]).astype(BF16)
        if k == 1:
            up, down, back, *rest = together(up, down, back, *rest)
            along = added(summed[0], back, *rest)
            far_keys = z_swap(along[1].astype(BF16))
        if k == 0:
            up, down, far_terms = together(up, down, far_terms)
            halves = own_terms + far_terms.astype(F32)
            far_terms = y_swap(halves[1].astype(BF16), 1)
        if k == 2:
            up, down = together(up, down)
    block = added(z_shift(up, 1), down, ours[0], theirs[0]).astype(BF16)
    block, far_terms, far_keys = together(block, far_terms, far_keys)
    layer_out = halves[0] + far_terms.astype(F32)

    blocks = [lax.ppermute(block, "dp", [(i, i ^ k) for i in range(4)]) for k in (2, 1, 3)]
    blocks = [block, blocks[1], blocks[0], blocks[2]]
    final = along[0] + far_keys.astype(F32)
    weight_grad = call(spread_kernel, [place] + blocks, shape((1024, 256), F32), [], 1)
    return (
        layer_out[None],
        grad_query[None],
        final[:, :256][None],
        final[:, 256:][None],
        weight_grad,
    )


def solution(mesh):
    placed = (
        P("dp", "seq", "head"),
        P("dp", "seq", "head"),
        P("dp", "seq", "head"),
        P("dp", "seq", "head"),
        P("dp", "seq"),
        P("head", None),
    )
    return jax.shard_map(
        shards,
        mesh=mesh,
        in_specs=placed,
        out_specs=(
            P("dp", "seq", "head"),
            P("dp", "seq", "head"),
            P("dp", "seq", "head"),
            P("dp", "seq", "head"),
            P("head", "seq"),
        ),
        check_vma=False,
    )
```

profile of v0, /device:TPU:56, one launch (start us, length us, event | category | flops | bytes accessed | tf_op | source)
XLA Modules:
  0.0 123.8 jit_solution(432546163929286797)
XLA Ops:
  4.2 6.3 %collective-permute-start.2 = (bf16[144,512]{1,0:T(8,128)(2,1)}, bf16[144,512]{1,0:T(8,128)(2,1)S(1)}, u32[]{:S(2)}, u32[]{:S(2)}) collective-permute-start(bf16[144,512]{1,0:T(8,128)(2,1)} %shard_map.101), channel_id=1, source_target_pairs={{0,32},{4,36},{8,40},{12,44},{16,48},{20,52},{24,56},{28,60},{32,0... | collective-permute-start | bytes 442376 | tf_op jit(solution)/shard_map/ppermute | solution.py:38
  11.9 2.1 %collective-permute-start.4 = (bf16[144,512]{1,0:T(8,128)(2,1)}, bf16[144,512]{1,0:T(8,128)(2,1)S(1)}, u32[]{:S(2)}, u32[]{:S(2)}) collective-permute-start(bf16[144,512]{1,0:T(8,128)(2,1)} %shard_map.101), channel_id=1, source_target_pairs={{0,24},{4,28},{8,16},{12,20},{16,8},{20,12},{24,0},{28,4},{32,56},... | collective-permute-start | bytes 442376 | tf_op jit(solution)/shard_map/ppermute | solution.py:34
  15.0 2.0 %collective-permute-done.2 = bf16[144,512]{1,0:T(8,128)(2,1)S(1)} collective-permute-done((bf16[144,512]{1,0:T(8,128)(2,1)}, bf16[144,512]{1,0:T(8,128)(2,1)S(1)}, u32[]{:S(2)}, u32[]{:S(2)}) %collective-permute-start.2) | collective-permute-done | bytes 147488 | tf_op jit(solution)/shard_map/ppermute | solution.py:38
  17.0 3.0 %collective-permute-start.5 = (bf16[144,512]{1,0:T(8,128)(2,1)}, bf16[144,512]{1,0:T(8,128)(2,1)S(1)}, u32[]{:S(2)}, u32[]{:S(2)}) collective-permute-start(bf16[144,512]{1,0:T(8,128)(2,1)} %shard_map.101), channel_id=1, source_target_pairs={{0,16},{4,20},{8,24},{12,28},{16,0},{20,4},{24,8},{28,12},{32,48},... | collective-permute-start | bytes 442376 | tf_op jit(solution)/shard_map/ppermute | solution.py:34
  20.1 2.4 %collective-permute-start.9 = (bf16[128,1024]{1,0:T(8,128)(2,1)S(1)}, bf16[128,1024]{1,0:T(8,128)(2,1)S(1)}, u32[]{:S(2)}, u32[]{:S(2)}) collective-permute-start(bf16[128,1024]{1,0:T(8,128)(2,1)S(1)} %bitcast.98), channel_id=1, source_target_pairs={{0,2},{1,3},{2,0},{3,1},{4,6},{5,7},{6,4},{7,5},{8,10},{9,11},{10,... | collective-permute-start | bytes 786440 | tf_op jit(solution)/shard_map/ppermute | solution.py:270
  24.7 2.0 %collective-permute-start.8 = (bf16[144,512]{1,0:T(8,128)(2,1)S(1)}, bf16[144,512]{1,0:T(8,128)(2,1)S(1)}, u32[]{:S(2)}, u32[]{:S(2)}) collective-permute-start(bf16[144,512]{1,0:T(8,128)(2,1)S(1)} %collective-permute-done.2), channel_id=1, source_target_pairs={{0,16},{4,20},{8,24},{12,28},{16,0},{20,4},{24,8},{28,12},{32,48},... | collective-permute-start | bytes 442376 | tf_op jit(solution)/shard_map/ppermute | solution.py:34
  29.5 1.9 %collective-permute-done.8 = bf16[144,512]{1,0:T(8,128)(2,1)S(1)} collective-permute-done((bf16[144,512]{1,0:T(8,128)(2,1)S(1)}, bf16[144,512]{1,0:T(8,128)(2,1)S(1)}, u32[]{:S(2)}, u32[]{:S(2)}) %collective-permute-start.8) | collective-permute-done | bytes 147488 | tf_op jit(solution)/shard_map/ppermute | solution.py:34
  31.6 2.8 %collective-permute-done.10.refs_1_ = bf16[8,144,512]{2,1,0:T(8,128)(2,1)S(1)} collective-permute-done((bf16[8,144,512]{2,1,0:T(8,128)(2,1)S(1)}, bf16[8,144,512]{2,1,0:T(8,128)(2,1)S(1)}, u32[]{:S(2)}, u32[]{:S(2)}) %collective-permute-start.10) | collective-permute-done | bytes 1179680 | tf_op jit(solution)/shard_map/ppermute | solution.py:30
  38.5 5.7 %shard_map.104.d_ref = bf16[128,1024]{1,0:T(8,128)(2,1)S(1)} custom-call(s32[4]{0:T(128)S(1)} %pad_add_fusion.at_ref, bf16[128,1024]{1,0:T(8,128)(2,1)S(1)} %bitcast.100, bf16[128,1024]{1,0:T(8,128)(2,1)S(1)} %collective-permute-done.g1, bf16[128,1024]{1,0:T(8,128)(2,1)S(1)} %collective-permute-done.9.g2, bf16[128,1024]{1,0:T(8,128)(2,1)S(1)} %collective-permute-done.1.g3, ...), custom_call_target="tpu_custom_call" | custom-call | flops 35999997952 | bytes 1048576 | tf_op jit(solution)/shard_map/pallas_call | solution.py:256
  44.3 3.9 %shard_map.103 = (bf16[128,1024]{1,0:T(8,128)(2,1)S(1)}, f32[2,8,512]{2,1,0:T(8,128)S(1)}) custom-call(s32[1]{0:T(128)} %bitcast.own_ref, bf16[128,1024]{1,0:T(8,128)(2,1)S(1)} %bitcast.101, bf16[8,144,512]{2,1,0:T(8,128)(2,1)S(1)} %bitcast_dynamic-update-slice_fusion.refs_0_, bf16[8,144,512]{2,1,0:T(8,128)(2,1)S(1)} %collective-permute-done.10.refs_1_), custom_call_target="tpu_custom_call" | custom-call | flops 24000000000 | bytes 1048576 | tf_op jit(solution)/shard_map/pallas_call | solution.py:256
  54.5 6.2 %shard_map.105 = (f32[128,1024]{1,0:T(8,128)}, bf16[4,2,128,512]{3,2,1,0:T(8,128)(2,1)S(1)}, bf16[4,2,128,512]{3,2,1,0:T(8,128)(2,1)S(1)}) custom-call(s32[1]{0:T(128)} %bitcast.own_ref, bf16[128,1024]{1,0:T(8,128)(2,1)S(1)} %bitcast.102, bf16[128,1024]{1,0:T(8,128)(2,1)S(1)} %shard_map.104.d_ref, ...), custom_call_target="tpu_custom_call" | custom-call | flops 65999998976 | bytes 1048576 | tf_op jit(solution)/shard_map/pallas_call | solution.py:256
  60.7 4.5 %shard_map.106 = (f32[2,128,1024]{2,1,0:T(8,128)S(1)}, bf16[2,128,1024]{2,1,0:T(8,128)(2,1)S(1)}) custom-call(s32[4]{0:T(128)S(1)} %pad_add_fusion.at_ref, bf16[128,1024]{1,0:T(8,128)(2,1)S(1)} %get-tuple-element.91.o_ref.h_ref.refs_0_, bf16[1024,4096]{1,0:T(8,128)(2,1)} %w_ref.3), custom_call_target="tpu_custom_call" | custom-call | flops 30000001024 | bytes 1048576 | tf_op jit(solution)/shard_map/pallas_call | solution.py:256
  69.6 1.9 %collective-permute-start.19 = (bf16[256,256]{1,0:T(8,128)(2,1)S(1)}, bf16[256,256]{1,0:T(8,128)(2,1)S(1)}, u32[]{:S(2)}, u32[]{:S(2)}) collective-permute-start(bf16[256,256]{1,0:T(8,128)(2,1)S(1)} %get-tuple-element.130), channel_id=1, source_target_pairs={{0,64},{4,68},{8,72},{12,76},{16,80},{20,84},{24,88},{28,92},{64,1... | collective-permute-start | bytes 393224 | tf_op jit(solution)/shard_map/ppermute | solution.py:279
  75.2 2.0 %collective-permute-start.26 = (bf16[2,128,512]{2,1,0:T(8,128)(2,1)S(1)}, bf16[2,128,512]{2,1,0:T(8,128)(2,1)S(1)}, u32[]{:S(2)}, u32[]{:S(2)}) collective-permute-start(bf16[2,128,512]{2,1,0:T(8,128)(2,1)S(1)} %get-tuple-element.131), channel_id=1, source_target_pairs={{0,16},{4,20},{8,24},{12,28},{16,0},{20,4},{24,8},{28,12},{32,48},... | collective-permute-start | bytes 786440 | tf_op jit(solution)/shard_map/ppermute | solution.py:34
  77.3 4.8 %collective-permute-done.21 = bf16[2,128,1024]{2,1,0:T(8,128)(2,1)S(1)} collective-permute-done((bf16[2,128,1024]{2,1,0:T(8,128)(2,1)S(1)}, bf16[2,128,1024]{2,1,0:T(8,128)(2,1)S(1)}, u32[]{:S(2)}, u32[]{:S(2)}) %collective-permute-start.21) | collective-permute-done | bytes 524320 | tf_op jit(solution)/shard_map/ppermute | solution.py:270
  82.0 1.8 %collective-permute-start.22 = (bf16[256,256]{1,0:T(8,128)(2,1)S(1)}, bf16[256,256]{1,0:T(8,128)(2,1)S(1)}, u32[]{:S(2)}, u32[]{:S(2)}) collective-permute-start(bf16[256,256]{1,0:T(8,128)(2,1)S(1)} %get-tuple-element.111), channel_id=1, source_target_pairs={{0,64},{4,68},{8,72},{12,76},{16,80},{20,84},{24,88},{28,92},{64,1... | collective-permute-start | bytes 393224 | tf_op jit(solution)/shard_map/ppermute | solution.py:279
  84.3 2.7 %collective-permute-done.22 = bf16[256,256]{1,0:T(8,128)(2,1)S(1)} collective-permute-done((bf16[256,256]{1,0:T(8,128)(2,1)S(1)}, bf16[256,256]{1,0:T(8,128)(2,1)S(1)}, u32[]{:S(2)}, u32[]{:S(2)}) %collective-permute-start.22) | collective-permute-done | bytes 131104 | tf_op jit(solution)/shard_map/ppermute | solution.py:279
  89.0 1.8 %collective-permute-start.27 = (bf16[256,256]{1,0:T(8,128)(2,1)S(1)}, bf16[256,256]{1,0:T(8,128)(2,1)S(1)}, u32[]{:S(2)}, u32[]{:S(2)}) collective-permute-start(bf16[256,256]{1,0:T(8,128)(2,1)S(1)} %get-tuple-element.114), channel_id=1, source_target_pairs={{0,64},{4,68},{8,72},{12,76},{16,80},{20,84},{24,88},{28,92},{64,1... | collective-permute-start | bytes 393224 | tf_op jit(solution)/shard_map/ppermute | solution.py:279
  91.2 2.8 %collective-permute-done.27 = bf16[256,256]{1,0:T(8,128)(2,1)S(1)} collective-permute-done((bf16[256,256]{1,0:T(8,128)(2,1)S(1)}, bf16[256,256]{1,0:T(8,128)(2,1)S(1)}, u32[]{:S(2)}, u32[]{:S(2)}) %collective-permute-start.27) | collective-permute-done | bytes 131104 | tf_op jit(solution)/shard_map/ppermute | solution.py:279
  94.1 2.9 %collective-permute-done.28 = bf16[256,256]{1,0:T(8,128)(2,1)S(1)} collective-permute-done((bf16[256,256]{1,0:T(8,128)(2,1)S(1)}, bf16[256,256]{1,0:T(8,128)(2,1)S(1)}, u32[]{:S(2)}, u32[]{:S(2)}) %collective-permute-start.28) | collective-permute-done | bytes 131104 | tf_op jit(solution)/shard_map/ppermute | solution.py:279
  96.9 2.0 %collective-permute-start.29 = (bf16[256,256]{1,0:T(8,128)(2,1)S(1)}, bf16[256,256]{1,0:T(8,128)(2,1)S(1)}, u32[]{:S(2)}, u32[]{:S(2)}) collective-permute-start(bf16[256,256]{1,0:T(8,128)(2,1)S(1)} %fusion.7), channel_id=1, source_target_pairs={{0,64},{4,68},{8,72},{12,76},{16,80},{20,84},{24,88},{28,92},{64,1... | collective-permute-start | bytes 393224 | tf_op jit(solution)/shard_map/ppermute | solution.py:279
  102.0 10.1 %collective-permute-done.31 = bf16[128,512]{1,0:T(8,128)(2,1)S(1)} collective-permute-done((bf16[128,512]{1,0:T(8,128)(2,1)S(1)}, bf16[128,512]{1,0:T(8,128)(2,1)S(1)}, u32[]{:S(2)}, u32[]{:S(2)}) %collective-permute-start.31) | collective-permute-done | bytes 131104 | tf_op jit(solution)/shard_map/ppermute | solution.py:38
  113.3 2.3 %collective-permute-start.34 = (bf16[256,256]{1,0:T(8,128)(2,1)S(1)}, bf16[256,256]{1,0:T(8,128)(2,1)S(1)}, u32[]{:S(2)}, u32[]{:S(2)}) collective-permute-start(bf16[256,256]{1,0:T(8,128)(2,1)S(1)} %fusion.6.p0), channel_id=1, source_target_pairs={{0,192},{64,128},{128,64},{192,0},{1,193},{65,129},{129,65},{193,1... | collective-permute-start | bytes 393224 | tf_op jit(solution)/shard_map/ppermute | solution.py:402
  118.1 4.1 %collective-permute-done.34.p3 = bf16[256,256]{1,0:T(8,128)(2,1)S(1)} collective-permute-done((bf16[256,256]{1,0:T(8,128)(2,1)S(1)}, bf16[256,256]{1,0:T(8,128)(2,1)S(1)}, u32[]{:S(2)}, u32[]{:S(2)}) %collective-permute-start.34) | collective-permute-done | bytes 131104 | tf_op jit(solution)/shard_map/ppermute | solution.py:402
  (92 shorter events, 40.9 us)
Async XLA Ops:
  2.3 17.8 %collective-permute-start = (bf16[128,1024]{1,0:T(8,128)(2,1)S(1)}, bf16[128,1024]{1,0:T(8,128)(2,1)S(1)}, u32[]{:S(2)}, u32[]{:S(2)}) collective-permute-start(bf16[128,1024]{1,0:T(8,128)(2,1)S(1)} %bitcast.96), channel_id=1, source_target_pairs={{0,1},{1,0},{2,3},{3,2},{4,5},{5,4},{6,7},{7,6},{8,9},{9,8},{10,11... | collective-permute-start | bytes 786440 | tf_op jit(solution)/shard_map/ppermute | solution.py:270
  3.1 17.0 %collective-permute-start.1 = (bf16[128,1024]{1,0:T(8,128)(2,1)S(1)}, bf16[128,1024]{1,0:T(8,128)(2,1)S(1)}, u32[]{:S(2)}, u32[]{:S(2)}) collective-permute-start(bf16[128,1024]{1,0:T(8,128)(2,1)S(1)} %bitcast.97), channel_id=1, source_target_pairs={{0,3},{1,2},{2,1},{3,0},{4,7},{5,6},{6,5},{7,4},{8,11},{9,10},{10,... | collective-permute-start | bytes 786440 | tf_op jit(solution)/shard_map/ppermute | solution.py:270
  4.2 12.8 %collective-permute-start.2 = (bf16[144,512]{1,0:T(8,128)(2,1)}, bf16[144,512]{1,0:T(8,128)(2,1)S(1)}, u32[]{:S(2)}, u32[]{:S(2)}) collective-permute-start(bf16[144,512]{1,0:T(8,128)(2,1)} %shard_map.101), channel_id=1, source_target_pairs={{0,32},{4,36},{8,40},{12,44},{16,48},{20,52},{24,56},{28,60},{32,0... | collective-permute-start | bytes 442376 | tf_op jit(solution)/shard_map/ppermute | solution.py:38
  10.4 9.6 %collective-permute-start.3 = (bf16[144,512]{1,0:T(8,128)(2,1)}, bf16[144,512]{1,0:T(8,128)(2,1)S(1)}, u32[]{:S(2)}, u32[]{:S(2)}) collective-permute-start(bf16[144,512]{1,0:T(8,128)(2,1)} %shard_map.101), channel_id=1, source_target_pairs={{0,8},{4,12},{8,0},{12,4},{16,24},{20,28},{24,16},{28,20},{32,40},... | collective-permute-start | bytes 442376 | tf_op jit(solution)/shard_map/ppermute | solution.py:34
  11.9 8.1 %collective-permute-start.4 = (bf16[144,512]{1,0:T(8,128)(2,1)}, bf16[144,512]{1,0:T(8,128)(2,1)S(1)}, u32[]{:S(2)}, u32[]{:S(2)}) collective-permute-start(bf16[144,512]{1,0:T(8,128)(2,1)} %shard_map.101), channel_id=1, source_target_pairs={{0,24},{4,28},{8,16},{12,20},{16,8},{20,12},{24,0},{28,4},{32,56},... | collective-permute-start | bytes 442376 | tf_op jit(solution)/shard_map/ppermute | solution.py:34
  17.0 11.8 %collective-permute-start.5 = (bf16[144,512]{1,0:T(8,128)(2,1)}, bf16[144,512]{1,0:T(8,128)(2,1)S(1)}, u32[]{:S(2)}, u32[]{:S(2)}) collective-permute-start(bf16[144,512]{1,0:T(8,128)(2,1)} %shard_map.101), channel_id=1, source_target_pairs={{0,16},{4,20},{8,24},{12,28},{16,0},{20,4},{24,8},{28,12},{32,48},... | collective-permute-start | bytes 442376 | tf_op jit(solution)/shard_map/ppermute | solution.py:34
  20.1 7.9 %collective-permute-start.9 = (bf16[128,1024]{1,0:T(8,128)(2,1)S(1)}, bf16[128,1024]{1,0:T(8,128)(2,1)S(1)}, u32[]{:S(2)}, u32[]{:S(2)}) collective-permute-start(bf16[128,1024]{1,0:T(8,128)(2,1)S(1)} %bitcast.98), channel_id=1, source_target_pairs={{0,2},{1,3},{2,0},{3,1},{4,6},{5,7},{6,4},{7,5},{8,10},{9,11},{10,... | collective-permute-start | bytes 786440 | tf_op jit(solution)/shard_map/ppermute | solution.py:270
  22.5 6.3 %collective-permute-start.6 = (bf16[144,512]{1,0:T(8,128)(2,1)S(1)}, bf16[144,512]{1,0:T(8,128)(2,1)S(1)}, u32[]{:S(2)}, u32[]{:S(2)}) collective-permute-start(bf16[144,512]{1,0:T(8,128)(2,1)S(1)} %collective-permute-done.2), channel_id=1, source_target_pairs={{0,8},{4,12},{8,0},{12,4},{16,24},{20,28},{24,16},{28,20},{32,40},... | collective-permute-start | bytes 442376 | tf_op jit(solution)/shard_map/ppermute | solution.py:34
  23.1 6.4 %collective-permute-start.7 = (bf16[144,512]{1,0:T(8,128)(2,1)S(1)}, bf16[144,512]{1,0:T(8,128)(2,1)S(1)}, u32[]{:S(2)}, u32[]{:S(2)}) collective-permute-start(bf16[144,512]{1,0:T(8,128)(2,1)S(1)} %collective-permute-done.2), channel_id=1, source_target_pairs={{0,24},{4,28},{8,16},{12,20},{16,8},{20,12},{24,0},{28,4},{32,56},... | collective-permute-start | bytes 442376 | tf_op jit(solution)/shard_map/ppermute | solution.py:34
  24.7 6.6 %collective-permute-start.8 = (bf16[144,512]{1,0:T(8,128)(2,1)S(1)}, bf16[144,512]{1,0:T(8,128)(2,1)S(1)}, u32[]{:S(2)}, u32[]{:S(2)}) collective-permute-start(bf16[144,512]{1,0:T(8,128)(2,1)S(1)} %collective-permute-done.2), channel_id=1, source_target_pairs={{0,16},{4,20},{8,24},{12,28},{16,0},{20,4},{24,8},{28,12},{32,48},... | collective-permute-start | bytes 442376 | tf_op jit(solution)/shard_map/ppermute | solution.py:34
  34.4 15.4 %collective-permute-start.11 = (bf16[2,2,128,256]{3,2,1,0:T(8,128)(2,1)}, bf16[2,2,128,256]{3,2,1,0:T(8,128)(2,1)S(1)}, u32[]{:S(2)}, u32[]{:S(2)}) collective-permute-start(bf16[2,2,128,256]{3,2,1,0:T(8,128)(2,1)} %copy-done.4), channel_id=1, source_target_pairs={{0,24},{4,28},{8,16},{12,20},{16,8},{20,12},{24,0},{28,4},{32,56},... | collective-permute-start | bytes 786440 | tf_op jit(solution)/shard_map/ppermute | solution.py:34
  36.1 13.7 %collective-permute-start.12 = (bf16[2,2,128,256]{3,2,1,0:T(8,128)(2,1)}, bf16[2,2,128,256]{3,2,1,0:T(8,128)(2,1)S(1)}, u32[]{:S(2)}, u32[]{:S(2)}) collective-permute-start(bf16[2,2,128,256]{3,2,1,0:T(8,128)(2,1)} %copy-done.3), channel_id=1, source_target_pairs={{0,16},{4,20},{8,24},{12,28},{16,0},{20,4},{24,8},{28,12},{32,48},... | collective-permute-start | bytes 786440 | tf_op jit(solution)/shard_map/ppermute | solution.py:34
  37.8 12.6 %collective-permute-start.13 = (bf16[2,2,128,256]{3,2,1,0:T(8,128)(2,1)}, bf16[2,2,128,256]{3,2,1,0:T(8,128)(2,1)S(1)}, u32[]{:S(2)}, u32[]{:S(2)}) collective-permute-start(bf16[2,2,128,256]{3,2,1,0:T(8,128)(2,1)} %copy-done.2), channel_id=1, source_target_pairs={{0,8},{4,12},{8,0},{12,4},{16,24},{20,28},{24,16},{28,20},{32,40},... | collective-permute-start | bytes 786440 | tf_op jit(solution)/shard_map/ppermute | solution.py:34
  50.4 14.8 %collective-permute-start.14 = (bf16[128,1024]{1,0:T(8,128)(2,1)S(1)}, bf16[128,1024]{1,0:T(8,128)(2,1)S(1)}, u32[]{:S(2)}, u32[]{:S(2)}) collective-permute-start(bf16[128,1024]{1,0:T(8,128)(2,1)S(1)} %get-tuple-element.91.o_ref.h_ref.refs_0_), channel_id=1, source_target_pairs={{0,24},{4,28},{8,16},{12,20},{16,8},{20,12},{24,0},{28,4},{32,56},... | collective-permute-start | bytes 786440 | tf_op jit(solution)/shard_map/ppermute | solution.py:34
  52.1 13.2 %collective-permute-start.15 = (bf16[128,1024]{1,0:T(8,128)(2,1)S(1)}, bf16[128,1024]{1,0:T(8,128)(2,1)S(1)}, u32[]{:S(2)}, u32[]{:S(2)}) collective-permute-start(bf16[128,1024]{1,0:T(8,128)(2,1)S(1)} %get-tuple-element.91.o_ref.h_ref.refs_0_), channel_id=1, source_target_pairs={{0,16},{4,20},{8,24},{12,28},{16,0},{20,4},{24,8},{28,12},{32,48},... | collective-permute-start | bytes 786440 | tf_op jit(solution)/shard_map/ppermute | solution.py:34
  53.8 11.5 %collective-permute-start.16 = (bf16[128,1024]{1,0:T(8,128)(2,1)S(1)}, bf16[128,1024]{1,0:T(8,128)(2,1)S(1)}, u32[]{:S(2)}, u32[]{:S(2)}) collective-permute-start(bf16[128,1024]{1,0:T(8,128)(2,1)S(1)} %get-tuple-element.91.o_ref.h_ref.refs_0_), channel_id=1, source_target_pairs={{0,8},{4,12},{8,0},{12,4},{16,24},{20,28},{24,16},{28,20},{32,40},... | collective-permute-start | bytes 786440 | tf_op jit(solution)/shard_map/ppermute | solution.py:34
  66.9 15.1 %collective-permute-start.21 = (bf16[2,128,1024]{2,1,0:T(8,128)(2,1)S(1)}, bf16[2,128,1024]{2,1,0:T(8,128)(2,1)S(1)}, u32[]{:S(2)}, u32[]{:S(2)}) collective-permute-start(bf16[2,128,1024]{2,1,0:T(8,128)(2,1)S(1)} %get-tuple-element.109), channel_id=1, source_target_pairs={{0,3},{1,2},{2,1},{3,0},{4,7},{5,6},{6,5},{7,4},{8,11},{9,10},{10,... | collective-permute-start | bytes 1572872 | tf_op jit(solution)/shard_map/ppermute | solution.py:270
  71.8 17.1 %collective-permute-start.24 = (bf16[2,128,512]{2,1,0:T(8,128)(2,1)S(1)}, bf16[2,128,512]{2,1,0:T(8,128)(2,1)S(1)}, u32[]{:S(2)}, u32[]{:S(2)}) collective-permute-start(bf16[2,128,512]{2,1,0:T(8,128)(2,1)S(1)} %get-tuple-element.133), channel_id=1, source_target_pairs={{0,8},{4,12},{8,0},{12,4},{16,24},{20,28},{24,16},{28,20},{32,40},... | collective-permute-start | bytes 786440 | tf_op jit(solution)/shard_map/ppermute | solution.py:34
  73.2 15.7 %collective-permute-start.25 = (bf16[2,128,512]{2,1,0:T(8,128)(2,1)S(1)}, bf16[2,128,512]{2,1,0:T(8,128)(2,1)S(1)}, u32[]{:S(2)}, u32[]{:S(2)}) collective-permute-start(bf16[2,128,512]{2,1,0:T(8,128)(2,1)S(1)} %get-tuple-element.132), channel_id=1, source_target_pairs={{0,24},{4,28},{8,16},{12,20},{16,8},{20,12},{24,0},{28,4},{32,56},... | collective-permute-start | bytes 786440 | tf_op jit(solution)/shard_map/ppermute | solution.py:34
  75.2 13.7 %collective-permute-start.26 = (bf16[2,128,512]{2,1,0:T(8,128)(2,1)S(1)}, bf16[2,128,512]{2,1,0:T(8,128)(2,1)S(1)}, u32[]{:S(2)}, u32[]{:S(2)}) collective-permute-start(bf16[2,128,512]{2,1,0:T(8,128)(2,1)S(1)} %get-tuple-element.131), channel_id=1, source_target_pairs={{0,16},{4,20},{8,24},{12,28},{16,0},{20,4},{24,8},{28,12},{32,48},... | collective-permute-start | bytes 786440 | tf_op jit(solution)/shard_map/ppermute | solution.py:34
  87.0 25.1 %collective-permute-start.30 = (bf16[128,1024]{1,0:T(8,128)(2,1)S(1)}, bf16[128,1024]{1,0:T(8,128)(2,1)S(1)}, u32[]{:S(2)}, u32[]{:S(2)}) collective-permute-start(bf16[128,1024]{1,0:T(8,128)(2,1)S(1)} %fusion.4), channel_id=1, source_target_pairs={{0,1},{1,0},{2,3},{3,2},{4,5},{5,4},{6,7},{7,6},{8,9},{9,8},{10,11... | collective-permute-start | bytes 786440 | tf_op jit(solution)/shard_map/ppermute | solution.py:270
  90.8 6.2 %collective-permute-start.28 = (bf16[256,256]{1,0:T(8,128)(2,1)S(1)}, bf16[256,256]{1,0:T(8,128)(2,1)S(1)}, u32[]{:S(2)}, u32[]{:S(2)}) collective-permute-start(bf16[256,256]{1,0:T(8,128)(2,1)S(1)} %get-tuple-element.115), channel_id=1, source_target_pairs={{0,224},{4,228},{8,232},{12,236},{16,240},{20,244},{24,248},{28,25... | collective-permute-start | bytes 393224 | tf_op jit(solution)/shard_map/ppermute | solution.py:279
  99.0 13.1 %collective-permute-start.31 = (bf16[128,512]{1,0:T(8,128)(2,1)S(1)}, bf16[128,512]{1,0:T(8,128)(2,1)S(1)}, u32[]{:S(2)}, u32[]{:S(2)}) collective-permute-start(bf16[128,512]{1,0:T(8,128)(2,1)S(1)} %fusion.14), channel_id=1, source_target_pairs={{0,32},{4,36},{8,40},{12,44},{16,48},{20,52},{24,56},{28,60},{32,0... | collective-permute-start | bytes 393224 | tf_op jit(solution)/shard_map/ppermute | solution.py:38
  113.3 8.9 %collective-permute-start.34 = (bf16[256,256]{1,0:T(8,128)(2,1)S(1)}, bf16[256,256]{1,0:T(8,128)(2,1)S(1)}, u32[]{:S(2)}, u32[]{:S(2)}) collective-permute-start(bf16[256,256]{1,0:T(8,128)(2,1)S(1)} %fusion.6.p0), channel_id=1, source_target_pairs={{0,192},{64,128},{128,64},{192,0},{1,193},{65,129},{129,65},{193,1... | collective-permute-start | bytes 393224 | tf_op jit(solution)/shard_map/ppermute | solution.py:402
  (18 other events, 81.4 us)
where the time goes:
time: 124 us
  starting transfers between devices  48.5 us (39%)
  waiting for transfers between devices  44.3 us (36%)
  Pallas kernels  26.1 us (21%)
  other arithmetic  2 us (2%)
  local copies, waits for them, and re-layouts  1.91 us (2%)
    pallas_call x9, Pallas kernels, call(): pl.pallas_call(kernel, out_shape=out_shape, in_specs=specs, out_specs=jax...  26.1 us
    ppermute x15, starting transfers between devices, x_swap(): lax.ppermute(value, 'seq', seq_perm(lambda z, x, c: (z, x ^ bits, c)))  23.5 us
    ppermute x7, waiting for transfers between devices, z_shift(): return lax.ppermute(value, ('dp', 'seq'), pairs)  12.7 us
    ppermute x2, waiting for transfers between devices, z_swap(): return lax.ppermute(value, 'seq', seq_perm(lambda z, x, c: (1 - z, x, c)))  12.1 us
    ppermute x7, starting transfers between devices, z_shift(): return lax.ppermute(value, ('dp', 'seq'), pairs)  8.25 us
    ppermute x2, starting transfers between devices, z_swap(): return lax.ppermute(value, 'seq', seq_perm(lambda z, x, c: (1 - z, x, c)))  7.45 us
    ppermute x5, waiting for transfers between devices, y_swap(): return lax.ppermute(value, 'head', [(i, i ^ bits) for i in range(4)])  6.14 us
    ppermute x5, starting transfers between devices, y_swap(): return lax.ppermute(value, 'head', [(i, i ^ bits) for i in range(4)])  5 us
  transfers between devices with their start and end apart: 35, of which 19 were waited for; matrix products, arithmetic and copies ran while one was open for 3% of the time, Pallas kernels for 19%

commit v1 on v0

--- a/solution.py
+++ b/solution.py
@@ -399,8 +399,8 @@
     block, far_terms, far_keys = together(block, far_terms, far_keys)
     layer_out = halves[0] + far_terms.astype(F32)
 
-    blocks = [lax.ppermute(block, "dp", [(i, i ^ k) for i in range(4)]) for k in (2, 1, 3)]
-    blocks = [block, blocks[1], blocks[0], blocks[2]]
+    blocks = [lax.ppermute(block, "dp", [(i, i ^ k) for i in range(4)]) for k in (1, 2, 3)]
+    blocks = [block, *blocks]
     final = along[0] + far_keys.astype(F32)
     weight_grad = call(spread_kernel, [place] + blocks, shape((1024, 256), F32), [], 1)
     return (

time: 124 us -> 124 us (level)
  no operation moved by 1% of the time
where the time goes in v1:
time: 124 us
  starting transfers between devices  48.5 us (39%)
  waiting for transfers between devices  44.3 us (36%)
  Pallas kernels  26.1 us (21%)
  other arithmetic  2 us (2%)
  local copies, waits for them, and re-layouts  1.91 us (2%)
    pallas_call x9, Pallas kernels, call(): pl.pallas_call(kernel, out_shape=out_shape, in_specs=specs, out_specs=jax...  26.1 us
    ppermute x15, starting transfers between devices, x_swap(): lax.ppermute(value, 'seq', seq_perm(lambda z, x, c: (z, x ^ bits, c)))  23.5 us
    ppermute x7, waiting for transfers between devices, z_shift(): return lax.ppermute(value, ('dp', 'seq'), pairs)  12.7 us
    ppermute x2, waiting for transfers between devices, z_swap(): return lax.ppermute(value, 'seq', seq_perm(lambda z, x, c: (1 - z, x, c)))  12.1 us
    ppermute x7, starting transfers between devices, z_shift(): return lax.ppermute(value, ('dp', 'seq'), pairs)  8.25 us
    ppermute x2, starting transfers between devices, z_swap(): return lax.ppermute(value, 'seq', seq_perm(lambda z, x, c: (1 - z, x, c)))  7.45 us
    ppermute x5, waiting for transfers between devices, y_swap(): return lax.ppermute(value, 'head', [(i, i ^ bits) for i in range(4)])  6.14 us
    ppermute x5, starting transfers between devices, y_swap(): return lax.ppermute(value, 'head', [(i, i ^ bits) for i in range(4)])  5 us
  transfers between devices with their start and end apart: 35, of which 19 were waited for; matrix products, arithmetic and copies ran while one was open for 3% of the time, Pallas kernels for 19%

profile of v1, /device:TPU:56, one launch (start us, length us, event | category | flops | bytes accessed | tf_op | source)
XLA Modules:
  0.0 123.8 jit_solution(432546163929286797)
XLA Ops:
  4.2 6.3 %collective-permute-start.2 = (bf16[144,512]{1,0:T(8,128)(2,1)}, bf16[144,512]{1,0:T(8,128)(2,1)S(1)}, u32[]{:S(2)}, u32[]{:S(2)}) collective-permute-start(bf16[144,512]{1,0:T(8,128)(2,1)} %shard_map.101), channel_id=1, source_target_pairs={{0,32},{4,36},{8,40},{12,44},{16,48},{20,52},{24,56},{28,60},{32,0... | collective-permute-start | bytes 442376 | tf_op jit(solution)/shard_map/ppermute | solution.py:38
  11.9 2.1 %collective-permute-start.4 = (bf16[144,512]{1,0:T(8,128)(2,1)}, bf16[144,512]{1,0:T(8,128)(2,1)S(1)}, u32[]{:S(2)}, u32[]{:S(2)}) collective-permute-start(bf16[144,512]{1,0:T(8,128)(2,1)} %shard_map.101), channel_id=1, source_target_pairs={{0,24},{4,28},{8,16},{12,20},{16,8},{20,12},{24,0},{28,4},{32,56},... | collective-permute-start | bytes 442376 | tf_op jit(solution)/shard_map/ppermute | solution.py:34
  15.0 2.0 %collective-permute-done.2 = bf16[144,512]{1,0:T(8,128)(2,1)S(1)} collective-permute-done((bf16[144,512]{1,0:T(8,128)(2,1)}, bf16[144,512]{1,0:T(8,128)(2,1)S(1)}, u32[]{:S(2)}, u32[]{:S(2)}) %collective-permute-start.2) | collective-permute-done | bytes 147488 | tf_op jit(solution)/shard_map/ppermute | solution.py:38
  17.0 3.0 %collective-permute-start.5 = (bf16[144,512]{1,0:T(8,128)(2,1)}, bf16[144,512]{1,0:T(8,128)(2,1)S(1)}, u32[]{:S(2)}, u32[]{:S(2)}) collective-permute-start(bf16[144,512]{1,0:T(8,128)(2,1)} %shard_map.101), channel_id=1, source_target_pairs={{0,16},{4,20},{8,24},{12,28},{16,0},{20,4},{24,8},{28,12},{32,48},... | collective-permute-start | bytes 442376 | tf_op jit(solution)/shard_map/ppermute | solution.py:34
  20.1 2.4 %collective-permute-start.9 = (bf16[128,1024]{1,0:T(8,128)(2,1)S(1)}, bf16[128,1024]{1,0:T(8,128)(2,1)S(1)}, u32[]{:S(2)}, u32[]{:S(2)}) collective-permute-start(bf16[128,1024]{1,0:T(8,128)(2,1)S(1)} %bitcast.98), channel_id=1, source_target_pairs={{0,2},{1,3},{2,0},{3,1},{4,6},{5,7},{6,4},{7,5},{8,10},{9,11},{10,... | collective-permute-start | bytes 786440 | tf_op jit(solution)/shard_map/ppermute | solution.py:270
  24.7 2.0 %collective-permute-start.8 = (bf16[144,512]{1,0:T(8,128)(2,1)S(1)}, bf16[144,512]{1,0:T(8,128)(2,1)S(1)}, u32[]{:S(2)}, u32[]{:S(2)}) collective-permute-start(bf16[144,512]{1,0:T(8,128)(2,1)S(1)} %collective-permute-done.2), channel_id=1, source_target_pairs={{0,16},{4,20},{8,24},{12,28},{16,0},{20,4},{24,8},{28,12},{32,48},... | collective-permute-start | bytes 442376 | tf_op jit(solution)/shard_map/ppermute | solution.py:34
  29.5 1.9 %collective-permute-done.8 = bf16[144,512]{1,0:T(8,128)(2,1)S(1)} collective-permute-done((bf16[144,512]{1,0:T(8,128)(2,1)S(1)}, bf16[144,512]{1,0:T(8,128)(2,1)S(1)}, u32[]{:S(2)}, u32[]{:S(2)}) %collective-permute-start.8) | collective-permute-done | bytes 147488 | tf_op jit(solution)/shard_map/ppermute | solution.py:34
  31.6 2.8 %collective-permute-done.10.refs_1_ = bf16[8,144,512]{2,1,0:T(8,128)(2,1)S(1)} collective-permute-done((bf16[8,144,512]{2,1,0:T(8,128)(2,1)S(1)}, bf16[8,144,512]{2,1,0:T(8,128)(2,1)S(1)}, u32[]{:S(2)}, u32[]{:S(2)}) %collective-permute-start.10) | collective-permute-done | bytes 1179680 | tf_op jit(solution)/shard_map/ppermute | solution.py:30
  38.5 5.7 %shard_map.104.d_ref = bf16[128,1024]{1,0:T(8,128)(2,1)S(1)} custom-call(s32[4]{0:T(128)S(1)} %pad_add_fusion.at_ref, bf16[128,1024]{1,0:T(8,128)(2,1)S(1)} %bitcast.100, bf16[128,1024]{1,0:T(8,128)(2,1)S(1)} %collective-permute-done.g1, bf16[128,1024]{1,0:T(8,128)(2,1)S(1)} %collective-permute-done.9.g2, bf16[128,1024]{1,0:T(8,128)(2,1)S(1)} %collective-permute-done.1.g3, ...), custom_call_target="tpu_custom_call" | custom-call | flops 35999997952 | bytes 1048576 | tf_op jit(solution)/shard_map/pallas_call | solution.py:256
  44.3 3.9 %shard_map.103 = (bf16[128,1024]{1,0:T(8,128)(2,1)S(1)}, f32[2,8,512]{2,1,0:T(8,128)S(1)}) custom-call(s32[1]{0:T(128)} %bitcast.own_ref, bf16[128,1024]{1,0:T(8,128)(2,1)S(1)} %bitcast.101, bf16[8,144,512]{2,1,0:T(8,128)(2,1)S(1)} %bitcast_dynamic-update-slice_fusion.refs_0_, bf16[8,144,512]{2,1,0:T(8,128)(2,1)S(1)} %collective-permute-done.10.refs_1_), custom_call_target="tpu_custom_call" | custom-call | flops 24000000000 | bytes 1048576 | tf_op jit(solution)/shard_map/pallas_call | solution.py:256
  54.5 6.2 %shard_map.105 = (f32[128,1024]{1,0:T(8,128)}, bf16[4,2,128,512]{3,2,1,0:T(8,128)(2,1)S(1)}, bf16[4,2,128,512]{3,2,1,0:T(8,128)(2,1)S(1)}) custom-call(s32[1]{0:T(128)} %bitcast.own_ref, bf16[128,1024]{1,0:T(8,128)(2,1)S(1)} %bitcast.102, bf16[128,1024]{1,0:T(8,128)(2,1)S(1)} %shard_map.104.d_ref, ...), custom_call_target="tpu_custom_call" | custom-call | flops 65999998976 | bytes 1048576 | tf_op jit(solution)/shard_map/pallas_call | solution.py:256
  60.7 4.5 %shard_map.106 = (f32[2,128,1024]{2,1,0:T(8,128)S(1)}, bf16[2,128,1024]{2,1,0:T(8,128)(2,1)S(1)}) custom-call(s32[4]{0:T(128)S(1)} %pad_add_fusion.at_ref, bf16[128,1024]{1,0:T(8,128)(2,1)S(1)} %get-tuple-element.91.o_ref.h_ref.refs_0_, bf16[1024,4096]{1,0:T(8,128)(2,1)} %w_ref.3), custom_call_target="tpu_custom_call" | custom-call | flops 30000001024 | bytes 1048576 | tf_op jit(solution)/shard_map/pallas_call | solution.py:256
  69.6 1.9 %collective-permute-start.19 = (bf16[256,256]{1,0:T(8,128)(2,1)S(1)}, bf16[256,256]{1,0:T(8,128)(2,1)S(1)}, u32[]{:S(2)}, u32[]{:S(2)}) collective-permute-start(bf16[256,256]{1,0:T(8,128)(2,1)S(1)} %get-tuple-element.130), channel_id=1, source_target_pairs={{0,64},{4,68},{8,72},{12,76},{16,80},{20,84},{24,88},{28,92},{64,1... | collective-permute-start | bytes 393224 | tf_op jit(solution)/shard_map/ppermute | solution.py:279
  75.2 2.0 %collective-permute-start.26 = (bf16[2,128,512]{2,1,0:T(8,128)(2,1)S(1)}, bf16[2,128,512]{2,1,0:T(8,128)(2,1)S(1)}, u32[]{:S(2)}, u32[]{:S(2)}) collective-permute-start(bf16[2,128,512]{2,1,0:T(8,128)(2,1)S(1)} %get-tuple-element.131), channel_id=1, source_target_pairs={{0,16},{4,20},{8,24},{12,28},{16,0},{20,4},{24,8},{28,12},{32,48},... | collective-permute-start | bytes 786440 | tf_op jit(solution)/shard_map/ppermute | solution.py:34
  77.3 4.8 %collective-permute-done.21 = bf16[2,128,1024]{2,1,0:T(8,128)(2,1)S(1)} collective-permute-done((bf16[2,128,1024]{2,1,0:T(8,128)(2,1)S(1)}, bf16[2,128,1024]{2,1,0:T(8,128)(2,1)S(1)}, u32[]{:S(2)}, u32[]{:S(2)}) %collective-permute-start.21) | collective-permute-done | bytes 524320 | tf_op jit(solution)/shard_map/ppermute | solution.py:270
  82.0 1.8 %collective-permute-start.22 = (bf16[256,256]{1,0:T(8,128)(2,1)S(1)}, bf16[256,256]{1,0:T(8,128)(2,1)S(1)}, u32[]{:S(2)}, u32[]{:S(2)}) collective-permute-start(bf16[256,256]{1,0:T(8,128)(2,1)S(1)} %get-tuple-element.111), channel_id=1, source_target_pairs={{0,64},{4,68},{8,72},{12,76},{16,80},{20,84},{24,88},{28,92},{64,1... | collective-permute-start | bytes 393224 | tf_op jit(solution)/shard_map/ppermute | solution.py:279
  84.3 2.7 %collective-permute-done.22 = bf16[256,256]{1,0:T(8,128)(2,1)S(1)} collective-permute-done((bf16[256,256]{1,0:T(8,128)(2,1)S(1)}, bf16[256,256]{1,0:T(8,128)(2,1)S(1)}, u32[]{:S(2)}, u32[]{:S(2)}) %collective-permute-start.22) | collective-permute-done | bytes 131104 | tf_op jit(solution)/shard_map/ppermute | solution.py:279
  89.0 1.8 %collective-permute-start.27 = (bf16[256,256]{1,0:T(8,128)(2,1)S(1)}, bf16[256,256]{1,0:T(8,128)(2,1)S(1)}, u32[]{:S(2)}, u32[]{:S(2)}) collective-permute-start(bf16[256,256]{1,0:T(8,128)(2,1)S(1)} %get-tuple-element.114), channel_id=1, source_target_pairs={{0,64},{4,68},{8,72},{12,76},{16,80},{20,84},{24,88},{28,92},{64,1... | collective-permute-start | bytes 393224 | tf_op jit(solution)/shard_map/ppermute | solution.py:279
  91.2 2.8 %collective-permute-done.27 = bf16[256,256]{1,0:T(8,128)(2,1)S(1)} collective-permute-done((bf16[256,256]{1,0:T(8,128)(2,1)S(1)}, bf16[256,256]{1,0:T(8,128)(2,1)S(1)}, u32[]{:S(2)}, u32[]{:S(2)}) %collective-permute-start.27) | collective-permute-done | bytes 131104 | tf_op jit(solution)/shard_map/ppermute | solution.py:279
  94.1 2.9 %collective-permute-done.28 = bf16[256,256]{1,0:T(8,128)(2,1)S(1)} collective-permute-done((bf16[256,256]{1,0:T(8,128)(2,1)S(1)}, bf16[256,256]{1,0:T(8,128)(2,1)S(1)}, u32[]{:S(2)}, u32[]{:S(2)}) %collective-permute-start.28) | collective-permute-done | bytes 131104 | tf_op jit(solution)/shard_map/ppermute | solution.py:279
  96.9 2.0 %collective-permute-start.29 = (bf16[256,256]{1,0:T(8,128)(2,1)S(1)}, bf16[256,256]{1,0:T(8,128)(2,1)S(1)}, u32[]{:S(2)}, u32[]{:S(2)}) collective-permute-start(bf16[256,256]{1,0:T(8,128)(2,1)S(1)} %fusion.7), channel_id=1, source_target_pairs={{0,64},{4,68},{8,72},{12,76},{16,80},{20,84},{24,88},{28,92},{64,1... | collective-permute-start | bytes 393224 | tf_op jit(solution)/shard_map/ppermute | solution.py:279
  102.0 10.1 %collective-permute-done.31 = bf16[128,512]{1,0:T(8,128)(2,1)S(1)} collective-permute-done((bf16[128,512]{1,0:T(8,128)(2,1)S(1)}, bf16[128,512]{1,0:T(8,128)(2,1)S(1)}, u32[]{:S(2)}, u32[]{:S(2)}) %collective-permute-start.31) | collective-permute-done | bytes 131104 | tf_op jit(solution)/shard_map/ppermute | solution.py:38
  113.3 2.3 %collective-permute-start.34 = (bf16[256,256]{1,0:T(8,128)(2,1)S(1)}, bf16[256,256]{1,0:T(8,128)(2,1)S(1)}, u32[]{:S(2)}, u32[]{:S(2)}) collective-permute-start(bf16[256,256]{1,0:T(8,128)(2,1)S(1)} %fusion.6.p0), channel_id=1, source_target_pairs={{0,192},{64,128},{128,64},{192,0},{1,193},{65,129},{129,65},{193,1... | collective-permute-start | bytes 393224 | tf_op jit(solution)/shard_map/ppermute | solution.py:402
  118.1 4.1 %collective-permute-done.34.p3 = bf16[256,256]{1,0:T(8,128)(2,1)S(1)} collective-permute-done((bf16[256,256]{1,0:T(8,128)(2,1)S(1)}, bf16[256,256]{1,0:T(8,128)(2,1)S(1)}, u32[]{:S(2)}, u32[]{:S(2)}) %collective-permute-start.34) | collective-permute-done | bytes 131104 | tf_op jit(solution)/shard_map/ppermute | solution.py:402
  (92 shorter events, 40.9 us)
Async XLA Ops:
  2.3 17.8 %collective-permute-start = (bf16[128,1024]{1,0:T(8,128)(2,1)S(1)}, bf16[128,1024]{1,0:T(8,128)(2,1)S(1)}, u32[]{:S(2)}, u32[]{:S(2)}) collective-permute-start(bf16[128,1024]{1,0:T(8,128)(2,1)S(1)} %bitcast.96), channel_id=1, source_target_pairs={{0,1},{1,0},{2,3},{3,2},{4,5},{5,4},{6,7},{7,6},{8,9},{9,8},{10,11... | collective-permute-start | bytes 786440 | tf_op jit(solution)/shard_map/ppermute | solution.py:270
  3.1 17.0 %collective-permute-start.1 = (bf16[128,1024]{1,0:T(8,128)(2,1)S(1)}, bf16[128,1024]{1,0:T(8,128)(2,1)S(1)}, u32[]{:S(2)}, u32[]{:S(2)}) collective-permute-start(bf16[128,1024]{1,0:T(8,128)(2,1)S(1)} %bitcast.97), channel_id=1, source_target_pairs={{0,3},{1,2},{2,1},{3,0},{4,7},{5,6},{6,5},{7,4},{8,11},{9,10},{10,... | collective-permute-start | bytes 786440 | tf_op jit(solution)/shard_map/ppermute | solution.py:270
  4.2 12.8 %collective-permute-start.2 = (bf16[144,512]{1,0:T(8,128)(2,1)}, bf16[144,512]{1,0:T(8,128)(2,1)S(1)}, u32[]{:S(2)}, u32[]{:S(2)}) collective-permute-start(bf16[144,512]{1,0:T(8,128)(2,1)} %shard_map.101), channel_id=1, source_target_pairs={{0,32},{4,36},{8,40},{12,44},{16,48},{20,52},{24,56},{28,60},{32,0... | collective-permute-start | bytes 442376 | tf_op jit(solution)/shard_map/ppermute | solution.py:38
  10.4 9.6 %collective-permute-start.3 = (bf16[144,512]{1,0:T(8,128)(2,1)}, bf16[144,512]{1,0:T(8,128)(2,1)S(1)}, u32[]{:S(2)}, u32[]{:S(2)}) collective-permute-start(bf16[144,512]{1,0:T(8,128)(2,1)} %shard_map.101), channel_id=1, source_target_pairs={{0,8},{4,12},{8,0},{12,4},{16,24},{20,28},{24,16},{28,20},{32,40},... | collective-permute-start | bytes 442376 | tf_op jit(solution)/shard_map/ppermute | solution.py:34
  11.9 8.1 %collective-permute-start.4 = (bf16[144,512]{1,0:T(8,128)(2,1)}, bf16[144,512]{1,0:T(8,128)(2,1)S(1)}, u32[]{:S(2)}, u32[]{:S(2)}) collective-permute-start(bf16[144,512]{1,0:T(8,128)(2,1)} %shard_map.101), channel_id=1, source_target_pairs={{0,24},{4,28},{8,16},{12,20},{16,8},{20,12},{24,0},{28,4},{32,56},... | collective-permute-start | bytes 442376 | tf_op jit(solution)/shard_map/ppermute | solution.py:34
  17.0 11.8 %collective-permute-start.5 = (bf16[144,512]{1,0:T(8,128)(2,1)}, bf16[144,512]{1,0:T(8,128)(2,1)S(1)}, u32[]{:S(2)}, u32[]{:S(2)}) collective-permute-start(bf16[144,512]{1,0:T(8,128)(2,1)} %shard_map.101), channel_id=1, source_target_pairs={{0,16},{4,20},{8,24},{12,28},{16,0},{20,4},{24,8},{28,12},{32,48},... | collective-permute-start | bytes 442376 | tf_op jit(solution)/shard_map/ppermute | solution.py:34
  20.1 7.9 %collective-permute-start.9 = (bf16[128,1024]{1,0:T(8,128)(2,1)S(1)}, bf16[128,1024]{1,0:T(8,128)(2,1)S(1)}, u32[]{:S(2)}, u32[]{:S(2)}) collective-permute-start(bf16[128,1024]{1,0:T(8,128)(2,1)S(1)} %bitcast.98), channel_id=1, source_target_pairs={{0,2},{1,3},{2,0},{3,1},{4,6},{5,7},{6,4},{7,5},{8,10},{9,11},{10,... | collective-permute-start | bytes 786440 | tf_op jit(solution)/shard_map/ppermute | solution.py:270
  22.5 6.3 %collective-permute-start.6 = (bf16[144,512]{1,0:T(8,128)(2,1)S(1)}, bf16[144,512]{1,0:T(8,128)(2,1)S(1)}, u32[]{:S(2)}, u32[]{:S(2)}) collective-permute-start(bf16[144,512]{1,0:T(8,128)(2,1)S(1)} %collective-permute-done.2), channel_id=1, source_target_pairs={{0,8},{4,12},{8,0},{12,4},{16,24},{20,28},{24,16},{28,20},{32,40},... | collective-permute-start | bytes 442376 | tf_op jit(solution)/shard_map/ppermute | solution.py:34
  23.1 6.4 %collective-permute-start.7 = (bf16[144,512]{1,0:T(8,128)(2,1)S(1)}, bf16[144,512]{1,0:T(8,128)(2,1)S(1)}, u32[]{:S(2)}, u32[]{:S(2)}) collective-permute-start(bf16[144,512]{1,0:T(8,128)(2,1)S(1)} %collective-permute-done.2), channel_id=1, source_target_pairs={{0,24},{4,28},{8,16},{12,20},{16,8},{20,12},{24,0},{28,4},{32,56},... | collective-permute-start | bytes 442376 | tf_op jit(solution)/shard_map/ppermute | solution.py:34
  24.7 6.6 %collective-permute-start.8 = (bf16[144,512]{1,0:T(8,128)(2,1)S(1)}, bf16[144,512]{1,0:T(8,128)(2,1)S(1)}, u32[]{:S(2)}, u32[]{:S(2)}) collective-permute-start(bf16[144,512]{1,0:T(8,128)(2,1)S(1)} %collective-permute-done.2), channel_id=1, source_target_pairs={{0,16},{4,20},{8,24},{12,28},{16,0},{20,4},{24,8},{28,12},{32,48},... | collective-permute-start | bytes 442376 | tf_op jit(solution)/shard_map/ppermute | solution.py:34
  34.4 15.4 %collective-permute-start.11 = (bf16[2,2,128,256]{3,2,1,0:T(8,128)(2,1)}, bf16[2,2,128,256]{3,2,1,0:T(8,128)(2,1)S(1)}, u32[]{:S(2)}, u32[]{:S(2)}) collective-permute-start(bf16[2,2,128,256]{3,2,1,0:T(8,128)(2,1)} %copy-done.4), channel_id=1, source_target_pairs={{0,24},{4,28},{8,16},{12,20},{16,8},{20,12},{24,0},{28,4},{32,56},... | collective-permute-start | bytes 786440 | tf_op jit(solution)/shard_map/ppermute | solution.py:34
  36.1 13.7 %collective-permute-start.12 = (bf16[2,2,128,256]{3,2,1,0:T(8,128)(2,1)}, bf16[2,2,128,256]{3,2,1,0:T(8,128)(2,1)S(1)}, u32[]{:S(2)}, u32[]{:S(2)}) collective-permute-start(bf16[2,2,128,256]{3,2,1,0:T(8,128)(2,1)} %copy-done.3), channel_id=1, source_target_pairs={{0,16},{4,20},{8,24},{12,28},{16,0},{20,4},{24,8},{28,12},{32,48},... | collective-permute-start | bytes 786440 | tf_op jit(solution)/shard_map/ppermute | solution.py:34
  37.8 12.6 %collective-permute-start.13 = (bf16[2,2,128,256]{3,2,1,0:T(8,128)(2,1)}, bf16[2,2,128,256]{3,2,1,0:T(8,128)(2,1)S(1)}, u32[]{:S(2)}, u32[]{:S(2)}) collective-permute-start(bf16[2,2,128,256]{3,2,1,0:T(8,128)(2,1)} %copy-done.2), channel_id=1, source_target_pairs={{0,8},{4,12},{8,0},{12,4},{16,24},{20,28},{24,16},{28,20},{32,40},... | collective-permute-start | bytes 786440 | tf_op jit(solution)/shard_map/ppermute | solution.py:34
  50.4 14.8 %collective-permute-start.14 = (bf16[128,1024]{1,0:T(8,128)(2,1)S(1)}, bf16[128,1024]{1,0:T(8,128)(2,1)S(1)}, u32[]{:S(2)}, u32[]{:S(2)}) collective-permute-start(bf16[128,1024]{1,0:T(8,128)(2,1)S(1)} %get-tuple-element.91.o_ref.h_ref.refs_0_), channel_id=1, source_target_pairs={{0,24},{4,28},{8,16},{12,20},{16,8},{20,12},{24,0},{28,4},{32,56},... | collective-permute-start | bytes 786440 | tf_op jit(solution)/shard_map/ppermute | solution.py:34
  52.1 13.2 %collective-permute-start.15 = (bf16[128,1024]{1,0:T(8,128)(2,1)S(1)}, bf16[128,1024]{1,0:T(8,128)(2,1)S(1)}, u32[]{:S(2)}, u32[]{:S(2)}) collective-permute-start(bf16[128,1024]{1,0:T(8,128)(2,1)S(1)} %get-tuple-element.91.o_ref.h_ref.refs_0_), channel_id=1, source_target_pairs={{0,16},{4,20},{8,24},{12,28},{16,0},{20,4},{24,8},{28,12},{32,48},... | collective-permute-start | bytes 786440 | tf_op jit(solution)/shard_map/ppermute | solution.py:34
  53.8 11.5 %collective-permute-start.16 = (bf16[128,1024]{1,0:T(8,128)(2,1)S(1)}, bf16[128,1024]{1,0:T(8,128)(2,1)S(1)}, u32[]{:S(2)}, u32[]{:S(2)}) collective-permute-start(bf16[128,1024]{1,0:T(8,128)(2,1)S(1)} %get-tuple-element.91.o_ref.h_ref.refs_0_), channel_id=1, source_target_pairs={{0,8},{4,12},{8,0},{12,4},{16,24},{20,28},{24,16},{28,20},{32,40},... | collective-permute-start | bytes 786440 | tf_op jit(solution)/shard_map/ppermute | solution.py:34
  66.9 15.1 %collective-permute-start.21 = (bf16[2,128,1024]{2,1,0:T(8,128)(2,1)S(1)}, bf16[2,128,1024]{2,1,0:T(8,128)(2,1)S(1)}, u32[]{:S(2)}, u32[]{:S(2)}) collective-permute-start(bf16[2,128,1024]{2,1,0:T(8,128)(2,1)S(1)} %get-tuple-element.109), channel_id=1, source_target_pairs={{0,3},{1,2},{2,1},{3,0},{4,7},{5,6},{6,5},{7,4},{8,11},{9,10},{10,... | collective-permute-start | bytes 1572872 | tf_op jit(solution)/shard_map/ppermute | solution.py:270
  71.8 17.1 %collective-permute-start.24 = (bf16[2,128,512]{2,1,0:T(8,128)(2,1)S(1)}, bf16[2,128,512]{2,1,0:T(8,128)(2,1)S(1)}, u32[]{:S(2)}, u32[]{:S(2)}) collective-permute-start(bf16[2,128,512]{2,1,0:T(8,128)(2,1)S(1)} %get-tuple-element.133), channel_id=1, source_target_pairs={{0,8},{4,12},{8,0},{12,4},{16,24},{20,28},{24,16},{28,20},{32,40},... | collective-permute-start | bytes 786440 | tf_op jit(solution)/shard_map/ppermute | solution.py:34
  73.2 15.7 %collective-permute-start.25 = (bf16[2,128,512]{2,1,0:T(8,128)(2,1)S(1)}, bf16[2,128,512]{2,1,0:T(8,128)(2,1)S(1)}, u32[]{:S(2)}, u32[]{:S(2)}) collective-permute-start(bf16[2,128,512]{2,1,0:T(8,128)(2,1)S(1)} %get-tuple-element.132), channel_id=1, source_target_pairs={{0,24},{4,28},{8,16},{12,20},{16,8},{20,12},{24,0},{28,4},{32,56},... | collective-permute-start | bytes 786440 | tf_op jit(solution)/shard_map/ppermute | solution.py:34
  75.2 13.7 %collective-permute-start.26 = (bf16[2,128,512]{2,1,0:T(8,128)(2,1)S(1)}, bf16[2,128,512]{2,1,0:T(8,128)(2,1)S(1)}, u32[]{:S(2)}, u32[]{:S(2)}) collective-permute-start(bf16[2,128,512]{2,1,0:T(8,128)(2,1)S(1)} %get-tuple-element.131), channel_id=1, source_target_pairs={{0,16},{4,20},{8,24},{12,28},{16,0},{20,4},{24,8},{28,12},{32,48},... | collective-permute-start | bytes 786440 | tf_op jit(solution)/shard_map/ppermute | solution.py:34
  87.0 25.1 %collective-permute-start.30 = (bf16[128,1024]{1,0:T(8,128)(2,1)S(1)}, bf16[128,1024]{1,0:T(8,128)(2,1)S(1)}, u32[]{:S(2)}, u32[]{:S(2)}) collective-permute-start(bf16[128,1024]{1,0:T(8,128)(2,1)S(1)} %fusion.4), channel_id=1, source_target_pairs={{0,1},{1,0},{2,3},{3,2},{4,5},{5,4},{6,7},{7,6},{8,9},{9,8},{10,11... | collective-permute-start | bytes 786440 | tf_op jit(solution)/shard_map/ppermute | solution.py:270
  90.8 6.2 %collective-permute-start.28 = (bf16[256,256]{1,0:T(8,128)(2,1)S(1)}, bf16[256,256]{1,0:T(8,128)(2,1)S(1)}, u32[]{:S(2)}, u32[]{:S(2)}) collective-permute-start(bf16[256,256]{1,0:T(8,128)(2,1)S(1)} %get-tuple-element.115), channel_id=1, source_target_pairs={{0,224},{4,228},{8,232},{12,236},{16,240},{20,244},{24,248},{28,25... | collective-permute-start | bytes 393224 | tf_op jit(solution)/shard_map/ppermute | solution.py:279
  99.0 13.1 %collective-permute-start.31 = (bf16[128,512]{1,0:T(8,128)(2,1)S(1)}, bf16[128,512]{1,0:T(8,128)(2,1)S(1)}, u32[]{:S(2)}, u32[]{:S(2)}) collective-permute-start(bf16[128,512]{1,0:T(8,128)(2,1)S(1)} %fusion.14), channel_id=1, source_target_pairs={{0,32},{4,36},{8,40},{12,44},{16,48},{20,52},{24,56},{28,60},{32,0... | collective-permute-start | bytes 393224 | tf_op jit(solution)/shard_map/ppermute | solution.py:38
  113.3 8.9 %collective-permute-start.34 = (bf16[256,256]{1,0:T(8,128)(2,1)S(1)}, bf16[256,256]{1,0:T(8,128)(2,1)S(1)}, u32[]{:S(2)}, u32[]{:S(2)}) collective-permute-start(bf16[256,256]{1,0:T(8,128)(2,1)S(1)} %fusion.6.p0), channel_id=1, source_target_pairs={{0,192},{64,128},{128,64},{192,0},{1,193},{65,129},{129,65},{193,1... | collective-permute-start | bytes 393224 | tf_op jit(solution)/shard_map/ppermute | solution.py:402
  (18 other events, 81.4 us)
